TPU v7x, 512 devices: a whole 4x4x16 slice. The times are simulated.
512 devices in a mesh: tile: 64 (over z, x), member: 8 (over y, core).
Axes of the slice: x: 4, y: 4, z: 16, core: 2. Of those that a mesh axis runs over, the one named last changes fastest.
Arguments:
- cells: bfloat16 [8, 256, 4, 16, 256], P('member', 'tile'), may hold values from -6 to 6
- cotangent: bfloat16 [8, 256, 4, 16, 256], P('member', 'tile'), may hold values from -6 to 6
- slot_lats: int32 [64, 4], P('tile'), may hold values from 0 to 7, as said below
- slot_count: int32 [64], P('tile'), may hold values from 1 to 4, as said below
- kernel: float32 [7, 7, 256], replicated, may hold values from -0.875 to 0.875
- ln_gain: float32 [256], replicated, may hold values from 0.5 to 1.5
- w_in: bfloat16 [256, 1024], P(None, 'member'), may hold values from -0.375 to 0.375
- b_in: bfloat16 [1024], P('member'), may hold values from -4 to 4
- w_out: bfloat16 [1024, 256], P('member'), may hold values from -0.1875 to 0.1875
- layer_scale: float32 [256], replicated, may hold values from 0.5 to 1.5
Outputs:
- blocked: bfloat16 [8, 256, 4, 16, 256], P('member', 'tile')
- cell_grad: bfloat16 [8, 256, 4, 16, 256], P('member', 'tile')
- grad_in: float32 [256, 1024], P(None, 'member')
- grad_out: float32 [1024, 256], P('member')
- kernel_grad: float32 [7, 7, 256], replicated
Inputs may be any that keep to these rules, and one draw needn't show every extreme that they name: `slot_lats`: row t lists 4 different tile rows of the grid; its first slot_count[t] entries are the wet tiles of tile column t. `slot_count`: some tile column has 4 wet tiles.
All inputs are finite; a program needn't handle non-finite values.
Results may differ from a plain program's by a relative error of at most 0.01.
Values may be sent and summed in bfloat16 or wider, within the bound.
A program may use at most 64 MiB of HBM per device.

v0:
```python
import math

import jax
import jax.numpy as jnp
from jax import lax
from jax.sharding import PartitionSpec as P

GY = 8


epsilon = 1e-06


def padded_2(x, sides, width):
    for axis, dim in sides:
        size, length = (lax.axis_size(axis), x.shape[dim])
        up = [(i, (i + 1) % size) for i in range(size)]
        down = [(j, i) for i, j in up]
        last = lax.slice_in_dim(x, length - width, length, axis=dim)
        initial = lax.slice_in_dim(x, 0, width, axis=dim)
        before = lax.ppermute(last, axis, up)
        after = lax.ppermute(initial, axis, down)
        x = jnp.concatenate([before, x, after], axis=dim)
    return x


def gelu_parts(hidden):
    cumulative = 0.5 * (1.0 + lax.erf(hidden * 0.7071067811865476))
    density = jnp.exp(-0.5 * hidden * hidden) * 0.3989422804014327
    return (hidden * cumulative, cumulative + hidden * density)


def depthwise(padded, kernel, height, breadth, flipped):
    span = kernel.shape[0]
    axis_row = padded.ndim - 3
    total = jnp.zeros(padded.shape[:-3] + (height, breadth, padded.shape[-1]), jnp.float32)
    for row_tap in range(span):
        rows_cut = lax.slice_in_dim(padded, row_tap, row_tap + height, axis=axis_row)
        for col_tap in range(span):
            window = lax.slice_in_dim(rows_cut, col_tap, col_tap + breadth, axis=axis_row + 1)
            if flipped:
                weight = kernel[span - 1 - row_tap, span - 1 - col_tap]
            else:
                weight = kernel[row_tap, col_tap]
            total = total + window.astype(jnp.float32) * weight
    return total


def kernel_taps(padded, gradient, height, breadth, span, axes_sum):
    axis_row = padded.ndim - 3
    rows_list = []
    for row_tap in range(span):
        rows_cut = lax.slice_in_dim(padded, row_tap, row_tap + height, axis=axis_row)
        cols_list = []
        for col_tap in range(span):
            window = lax.slice_in_dim(rows_cut, col_tap, col_tap + breadth, axis=axis_row + 1)
            cols_list.append(jnp.sum(window.astype(jnp.float32) * gradient, axis=axes_sum))
        rows_list.append(jnp.stack(cols_list))
    return jnp.stack(rows_list)


def mixing(conv_out, cells, cotangent, live_rows, ln_gain, w_in, b_in, w_out, layer_scale):
    channels = conv_out.shape[-1]
    layout = conv_out.shape
    flattened = conv_out.reshape(-1, channels)
    center = flattened - jnp.mean(flattened, axis=-1, keepdims=True)
    inverse = lax.rsqrt(jnp.mean(center * center, axis=-1, keepdims=True) + epsilon)
    normed = center * inverse
    scaled = (normed * ln_gain).astype(jnp.bfloat16)
    hidden = jnp.dot(scaled, w_in, preferred_element_type=jnp.float32) + b_in.astype(jnp.float32)
    active, derivative = gelu_parts(hidden)
    active = active.astype(jnp.bfloat16)
    branch = jnp.dot(active, w_out, preferred_element_type=jnp.float32)
    blocked = (cells.reshape(-1, channels).astype(jnp.float32) + layer_scale * branch) * live_rows
    d_branch = (
        cotangent.reshape(-1, channels).astype(jnp.float32) * layer_scale * live_rows
    ).astype(jnp.bfloat16)
    d_active = jnp.dot(d_branch, w_out.T, preferred_element_type=jnp.float32)
    grad_out = jnp.dot(active.T, d_branch, preferred_element_type=jnp.float32)
    d_hidden = (d_active * derivative).astype(jnp.bfloat16)
    grad_in = jnp.dot(scaled.T, d_hidden, preferred_element_type=jnp.float32)
    d_normed = jnp.dot(d_hidden, w_in.T, preferred_element_type=jnp.float32) * ln_gain
    d_conv = inverse * (
        d_normed
        - jnp.mean(d_normed, axis=-1, keepdims=True)
        - normed * jnp.mean(d_normed * normed, axis=-1, keepdims=True)
    )
    return (
        blocked.astype(jnp.bfloat16).reshape(layout),
        d_conv.astype(jnp.bfloat16).reshape(layout),
        grad_in,
        grad_out,
    )


def place_rows(onehot, values, reach):
    column = jnp.einsum(
        "gs,mshwc->mghwc", onehot, values, preferred_element_type=jnp.float32
    ).astype(jnp.bfloat16)
    dims_all = column.shape
    column = column.reshape(dims_all[0], dims_all[1] * dims_all[2], dims_all[3], dims_all[4])
    return jnp.pad(column, ((0, 0), (reach, reach), (0, 0), (0, 0)))


def cut_slabs(padded, lats, height, reach):
    pieces = [
        lax.dynamic_slice_in_dim(padded, lats[index] * height, height + 2 * reach, 1)
        for index in range(lats.shape[0])
    ]
    return jnp.stack(pieces, axis=1)


def on_device(
    cells, cotangent, slot_lats, slot_count, kernel, ln_gain, w_in, b_in, w_out, layer_scale
):
    members, slot_total, height, tile_width, channels = cells.shape
    reach = kernel.shape[0] // 2
    lats = slot_lats.reshape(-1)
    slot_ids = jnp.arange(slot_total, dtype=jnp.int32)
    live = slot_ids < slot_count[0]
    live_mask = live[None, :, None, None, None]
    grid_rows = jnp.arange(GY, dtype=jnp.int32)
    own_place = ((grid_rows[:, None] == lats[None, :]) & live[None, :]).astype(jnp.bfloat16)
    full_in, full_out, full_bias = (
        lax.all_gather(w_in, "member", axis=1, tiled=True),
        lax.all_gather(w_out, "member", axis=0, tiled=True),
        lax.all_gather(b_in, "member", axis=0, tiled=True),
    )

    def surround(values):
        padded = place_rows(own_place, values, reach)
        widened = padded_2(padded, (("tile", 2),), reach)
        return cut_slabs(widened, lats, height, reach)

    slabs = surround(cells)
    conv_out = depthwise(slabs, kernel, height, tile_width, False)
    live_rows = (
        jnp.broadcast_to(live_mask, cells.shape[:-1] + (1,)).astype(jnp.float32).reshape(-1, 1)
    )
    blocked, d_conv, grad_in, grad_out = mixing(
        conv_out, cells, cotangent, live_rows, ln_gain, full_in, full_bias, full_out, layer_scale
    )
    back_slabs = surround(d_conv)
    back = depthwise(back_slabs, kernel, height, tile_width, True)
    cell_grad = jnp.where(live_mask, cotangent.astype(jnp.float32) + back, 0.0).astype(jnp.bfloat16)
    kernel_grad = kernel_taps(
        slabs, d_conv.astype(jnp.float32), height, tile_width, kernel.shape[0], (0, 1, 2, 3)
    )
    ff_local = w_in.shape[1]
    total_in, total_out, kernel_total = lax.psum(
        (grad_in, grad_out, kernel_grad), ("tile", "member")
    )
    offset = lax.axis_index("member") * ff_local
    part_in = lax.dynamic_slice_in_dim(total_in, offset, ff_local, 1)
    part_out = lax.dynamic_slice_in_dim(total_out, offset, ff_local, 0)
    cell_count = (
        members * lax.axis_size("member") * lax.axis_size("tile") * slot_total * height * tile_width
    )
    factor = 1.0 / math.sqrt(cell_count)
    return (blocked, cell_grad, part_in * factor, part_out * factor, kernel_total * factor)


def solution(mesh):
    placed = (
        P("member", "tile", None, None, None),
        P("member", "tile", None, None, None),
        P("tile", None),
        P("tile"),
        P(),
        P(),
        P(None, "member"),
        P("member"),
        P("member", None),
        P(),
    )
    return jax.shard_map(
        on_device,
        mesh=mesh,
        in_specs=placed,
        out_specs=(
            P("member", "tile", None, None, None),
            P("member", "tile", None, None, None),
            P(None, "member"),
            P("member", None),
            P(),
        ),
        check_vma=False,
    )
```

profile of v0, /device:TPU:1, one launch (start us, length us, event | category | flops | bytes accessed | tf_op | source)
XLA Modules:
  0.0 666.9 jit_solution(14845129347940472997)
XLA Ops:
  7.2 0.0 all-reduce.5.cloned.1.call-start
  7.9 0.0 copy-start.5
  7.9 0.6 copy-done.5
  8.5 1.2 fusion.1
  9.8 0.0 copy-start.4
  9.8 0.1 pad_slice_fusion.3
  9.9 0.0 copy-start.2
  9.9 4.1 collective-permute-start
  14.0 12.1 %collective-permute-start.1 = (bf16[1,38,3,256]{3,2,1,0:T(4,128)(2,1)S(1)}, bf16[1,38,3,256]{3,2,1,0:T(4,128)(2,1)S(1)}, u32[]{:S(2)}, u32[]{:S(2)}) collective-permute-start(bf16[1,38,3,256]{3,2,1,0:T(4,128)(2,1)S(1)} %get-tuple-element.72), channel_id=1, source_target_pairs={{8,0},{16,8},{24,16},{32,24},{40,32},{48,40},{56,48},{64,56},{72,6... | collective-permute-start | bytes 175112 | tf_op jit(solution)/shard_map/ppermute | solution.py:22
  26.1 0.0 copy-done.4
  26.2 0.1 broadcast_in_dim.12
  26.3 0.1 broadcast_in_dim.13
  26.4 0.0 copy-done.2
  26.4 0.0 copy-start.3
  26.4 14.1 %all_gather.9 = bf16[256,1024]{1,0:T(8,128)(2,1)S(1)} all-gather(bf16[256,128]{1,0:T(8,128)(2,1)S(1)} %copy-done.2), channel_id=1, replica_groups=mesh['tile'=64,'member'=8] {'member'}, dimensions={1}, use_global_device_ids=true | all-gather | bytes 589824 | tf_op jit(solution)/shard_map/all_gather | solution.py:125
  40.5 0.0 copy-done.3
  40.5 0.0 copy-start
  40.5 0.0 copy-start.7
  40.5 13.2 %all_gather.11 = bf16[1024,256]{1,0:T(8,128)(2,1)S(1)} all-gather(bf16[128,256]{1,0:T(8,128)(2,1)S(1)} %copy-done.3), channel_id=1, replica_groups=mesh['tile'=64,'member'=8] {'member'}, dimensions={0}, use_global_device_ids=true | all-gather | bytes 589824 | tf_op jit(solution)/shard_map/all_gather | solution.py:126
  53.7 0.0 copy-done
  53.7 0.0 copy-done.7
  53.7 0.1 fusion.108
  53.8 0.6 fusion.123
  57.0 0.0 copy-start.8
  57.1 0.6 copy-done.8
  57.7 9.6 %all-gather = bf16[8,1,128]{2,1,0:T(2,128)(2,1)S(1)} all-gather(bf16[1,1,128]{2,1,0:T(2,128)(2,1)S(1)} %bitcast.398), channel_id=1, replica_groups=mesh['tile'=64,'member'=8] {'member'}, dimensions={0}, use_global_device_ids=true | all-gather | bytes 2304 | tf_op jit(solution)/shard_map/all_gather | solution.py:127
  67.4 0.0 collective-permute-done
  67.4 0.0 collective-permute-done.1
  67.4 0.3 pad_maximum_fusion.2
  67.7 0.1 pad_maximum_fusion
  67.8 1.8 fusion.118
  69.6 0.1 div.15
  69.7 0.2 multiply_reduce_fusion.1
  69.9 0.0 copy-start.6
  69.9 0.1 rsqrt.12
  70.0 0.6 copy-done.6
  70.6 0.1 multiply_convert_fusion.2
  70.7 0.4 multiply_convert_fusion
  71.1 0.6 fusion
  71.7 0.5 fusion.117
  72.2 0.8 fusion.106
  72.9 0.4 fusion.70
  73.4 0.7 fusion.88
  74.1 1.3 fusion.124
  75.4 0.0 copy-start.1
  75.4 1.3 fusion.125
  76.7 0.0 copy-done.1
  76.7 1.0 fusion.5
  77.9 99.9 %psum.23 = f32[7,7,256]{2,1,0:T(8,128)S(1)} all-reduce(f32[7,7,256]{2,1,0:T(8,128)S(1)} %constant_dynamic-update-slice_fusion), channel_id=1, replica_groups=mesh['tile'=64,'member'=8] {'tile','member'}, use_global_device_ids=true, to_apply=%region_55.56 | all-reduce | flops 12544 | bytes 100352 | tf_op jit(solution)/shard_map/psum | solution.py:150
  177.8 0.3 fusion.2
  178.2 0.1 pad_slice_fusion.1
  178.3 1.9 collective-permute-start.2
  180.2 6.9 %collective-permute-start.3 = (bf16[1,38,3,256]{3,2,1,0:T(4,128)(2,1)S(1)}, bf16[1,38,3,256]{3,2,1,0:T(4,128)(2,1)S(1)}, u32[]{:S(2)}, u32[]{:S(2)}) collective-permute-start(bf16[1,38,3,256]{3,2,1,0:T(4,128)(2,1)S(1)} %get-tuple-element.70), channel_id=1, source_target_pairs={{8,0},{16,8},{24,16},{32,24},{40,32},{48,40},{56,48},{64,56},{72,6... | collective-permute-start | bytes 175112 | tf_op jit(solution)/shard_map/ppermute | solution.py:22
  187.1 0.0 all-reduce.5.cloned.1.call-update
  187.1 0.6 broadcast_multiply_fusion
  187.8 0.0 collective-permute-done.2
  187.8 0.6 collective-permute-done.3
  188.3 0.3 pad_maximum_fusion.3
  188.7 0.1 pad_maximum_fusion.1
  188.8 2.7 select_convert_fusion
  191.4 465.5 %all-reduce.5.cloned.1.call-done = (f32[256,1024]{1,0:T(8,128)}, f32[1024,256]{1,0:T(8,128)}) async-done(((f32[256,1024]{1,0:T(8,128)}, f32[1024,256]{1,0:T(8,128)}), (f32[256,1024]{1,0:T(8,128)}, f32[1024,256]{1,0:T(8,128)})) %all-reduce.5.cloned.1.call-update) | async-done | bytes 2097168 | tf_op jit(solution)/shard_map/psum | solution.py:150
  656.9 1.6 dynamic-slice_multiply_fusion.1
  658.5 1.6 dynamic-slice_multiply_fusion
  (29 shorter events, 0.6 us)
Async XLA Ops:
  7.2 649.8 %all-reduce.5.cloned.1.call-start = ((), (), s32[]{:S(2)}) async-start(), calls=%async_computation | async-start | bytes 4194304 | tf_op jit(solution)/shard_map/psum | solution.py:150
  7.9 0.7 copy-start.5
  9.8 16.3 %copy-start.4 = (f32[7,7,256]{2,1,0:T(8,128)S(1)}, f32[7,7,256]{2,1,0:T(8,128)}, u32[]{:S(2)}) copy-start(f32[7,7,256]{2,1,0:T(8,128)} %param.14) | copy-start | bytes 150532
  9.9 16.5 %copy-start.2 = (bf16[256,128]{1,0:T(8,128)(2,1)S(1)}, bf16[256,128]{1,0:T(8,128)(2,1)}, u32[]{:S(2)}) copy-start(bf16[256,128]{1,0:T(8,128)(2,1)} %param.16) | copy-start | bytes 196612
  9.9 57.4 %collective-permute-start = (bf16[1,38,3,256]{3,2,1,0:T(4,128)(2,1)S(1)}, bf16[1,38,3,256]{3,2,1,0:T(4,128)(2,1)S(1)}, u32[]{:S(2)}, u32[]{:S(2)}) collective-permute-start(bf16[1,38,3,256]{3,2,1,0:T(4,128)(2,1)S(1)} %get-tuple-element.71), channel_id=1, source_target_pairs={{0,8},{8,16},{16,24},{24,32},{32,40},{40,48},{48,56},{56,64},{64,7... | collective-permute-start | bytes 175112 | tf_op jit(solution)/shard_map/ppermute | solution.py:21
  14.0 53.4 %collective-permute-start.1 = (bf16[1,38,3,256]{3,2,1,0:T(4,128)(2,1)S(1)}, bf16[1,38,3,256]{3,2,1,0:T(4,128)(2,1)S(1)}, u32[]{:S(2)}, u32[]{:S(2)}) collective-permute-start(bf16[1,38,3,256]{3,2,1,0:T(4,128)(2,1)S(1)} %get-tuple-element.72), channel_id=1, source_target_pairs={{8,0},{16,8},{24,16},{32,24},{40,32},{48,40},{56,48},{64,56},{72,6... | collective-permute-start | bytes 175112 | tf_op jit(solution)/shard_map/ppermute | solution.py:22
  26.4 14.1 %copy-start.3 = (bf16[128,256]{1,0:T(8,128)(2,1)S(1)}, bf16[128,256]{1,0:T(8,128)(2,1)}, u32[]{:S(2)}) copy-start(bf16[128,256]{1,0:T(8,128)(2,1)} %param.18) | copy-start | bytes 196612
  40.5 13.2 %copy-start = (bf16[1,4,4,16,256]{4,3,2,1,0:T(8,128)(2,1)S(1)}, bf16[1,4,4,16,256]{4,3,2,1,0:T(8,128)(2,1)}, u32[]{:S(2)}) copy-start(bf16[1,4,4,16,256]{4,3,2,1,0:T(8,128)(2,1)} %param.11) | copy-start | bytes 393220
  40.5 13.2 %copy-start.7 = (f32[256]{0:T(256)S(1)}, f32[256]{0:T(256)}, u32[]{:S(2)}) copy-start(f32[256]{0:T(256)} %param.19) | copy-start | bytes 3076
  57.0 0.7 copy-start.8
  69.9 0.7 copy-start.6
  75.4 1.3 copy-start.1
  178.3 9.5 %collective-permute-start.2 = (bf16[1,38,3,256]{3,2,1,0:T(4,128)(2,1)S(1)}, bf16[1,38,3,256]{3,2,1,0:T(4,128)(2,1)S(1)}, u32[]{:S(2)}, u32[]{:S(2)}) collective-permute-start(bf16[1,38,3,256]{3,2,1,0:T(4,128)(2,1)S(1)} %get-tuple-element.69), channel_id=1, source_target_pairs={{0,8},{8,16},{16,24},{24,32},{32,40},{40,48},{48,56},{56,64},{64,7... | collective-permute-start | bytes 175112 | tf_op jit(solution)/shard_map/ppermute | solution.py:21
  180.2 8.1 %collective-permute-start.3 = (bf16[1,38,3,256]{3,2,1,0:T(4,128)(2,1)S(1)}, bf16[1,38,3,256]{3,2,1,0:T(4,128)(2,1)S(1)}, u32[]{:S(2)}, u32[]{:S(2)}) collective-permute-start(bf16[1,38,3,256]{3,2,1,0:T(4,128)(2,1)S(1)} %get-tuple-element.70), channel_id=1, source_target_pairs={{8,0},{16,8},{24,16},{32,24},{40,32},{48,40},{56,48},{64,56},{72,6... | collective-permute-start | bytes 175112 | tf_op jit(solution)/shard_map/ppermute | solution.py:22
Sparse Core Ops, SparseCore 0:
  187.2 469.6 all-reduce.4
where the time goes:
time: 667 us
  waiting for transfers between devices  466 us (70%)
  blocking collectives  137 us (21%)
  starting transfers between devices  25 us (4%)
  between operations  17.6 us (3%)
  other arithmetic  11.3 us (2%)
    psum x1, waiting for transfers between devices, on_device(): lax.psum((grad_in, grad_out, kernel_grad), ('tile', 'member'))  466 us
    psum x1, blocking collectives, on_device(): lax.psum((grad_in, grad_out, kernel_grad), ('tile', 'member'))  99.9 us
    ppermute x2, starting transfers between devices, padded_2(): after = lax.ppermute(initial, axis, down)  19 us
    all_gather x1, blocking collectives, on_device(): lax.all_gather(w_in, 'member', axis=1, tiled=True)  14.1 us
  transfers between devices with their start and end apart: 5, of which 2 were waited for; matrix products, arithmetic and copies ran while one was open for 1% of the time, Pallas kernels for 0%

commit v1 on v0

v1 whole, which is shorter than its diff:
```python
import functools
import math

import jax
import jax.numpy as jnp
from jax import lax
from jax.experimental import pallas as pl
from jax.experimental.pallas import tpu as pltpu
from jax.sharding import PartitionSpec as P

NZ, NX, NY, NC = 16, 4, 4, 2
NL, NH = 4, 4
SLOTS, GY, TH, TW, KS = 4, 8, 4, 16, 7
REACH = KS // 2
LEFT = 8
ROWS = GY * TH
EPSILON = 1e-06
MESH = pl.DeviceIdType.MESH
F32, BF16 = jnp.float32, jnp.bfloat16
ORDER = (0, 1, 3, 2)
PEERS = 1 + 15 + 3 + 3 + 3 + 9 + 2

VMEM_SCRATCH = dict(
    grid_x=((ROWS + 2 * REACH, 32, 256), F32),
    grid_d=((ROWS + 2 * REACH, 32, 256), F32),
    edge=((2, 96, 256), F32),
    edge_x_out=((2, 96, 256), BF16),
    edge_x_in=((2, 96, 256), BF16),
    edge_d_out=((2, 96, 256), BF16),
    edge_d_in=((2, 96, 256), BF16),
    wi=((NY, 256, 256), BF16),
    wo=((NY, 256, 256), BF16),
    bias_own=((8, 128), F32),
    bias=((NY, 8, 256), F32),
    normed=((SLOTS, TH, TW, 256), F32),
    inverse=((SLOTS, TH, TW, 128), F32),
    scaled=((SLOTS, TH, TW, 256), BF16),
    d_branch=((SLOTS, TH, TW, 256), BF16),
    branch=((256, 256), F32),
    d_normed=((256, 256), F32),
    d_conv=((SLOTS, TH, TW, 256), F32),
    g_in=((NY, 256, 256), BF16),
    g_out=((NY, 256, 256), BF16),
    core_in=((NY, 256, 128), BF16),
    core_out=((NY, 128, 256), BF16),
    piece=((NY, NX, 128, 128), BF16),
    piece_in=((NY * NX, 128, 128), BF16),
    low_out=((NL, 32, 128), BF16),
    low_in=((NL, 32, 128), BF16),
    high=((NH, 32, 128), BF16),
    full=((NX, NL, 32, 128), BF16),
    taps=((NC, NY, 16, 128), F32),
    taps_core=((NY, 16, 128), F32),
    taps_sum=((NY, 16, 128), F32),
    taps_plane=((NY * NX, 16, 128), F32),
    taps_low=((NL, 16, 128), F32),
    taps_high=((NH, 16, 128), F32),
    taps_full=((NY * NC, 16, 128), F32),
)
DMA_COUNTS = dict(
    ex=2, ed=2, wy=9, wc=12, gc=8, gp=16, gl=4, gh=4, gg=16, kc=1, kp=16, kl=4, kh=4, km=8
)
INPUTS = (
    "cells", "cot", "lats", "count", "kernel", "gain", "w_in", "b_in", "w_out", "scale"
)
OUTPUTS = ("blocked", "cell_grad", "grad_in", "grad_out", "kernel_grad")


class Refs:
    pass


def gelu_parts(hidden):
    cumulative = 0.5 * (1.0 + lax.erf(hidden * 0.7071067811865476))
    density = jnp.exp(-0.5 * hidden * hidden) * 0.3989422804014327
    return (hidden * cumulative, cumulative + hidden * density)


def dot(a, b, contract):
    return lax.dot_general(a, b, ((contract[0:1], contract[1:2]), ((), ())), preferred_element_type=F32)


def block_kernel(factor, *refs):
    r = Refs()
    names = INPUTS + OUTPUTS + tuple(VMEM_SCRATCH)
    for name, ref in zip(names, refs):
        setattr(r, name, ref)
    sems = {}
    rest = refs[len(names):]
    for index, name in enumerate(DMA_COUNTS):
        sems[name] = (rest[2 * index], rest[2 * index + 1])

    t, m = lax.axis_index("tile"), lax.axis_index("member")
    z, x, y, c = t // NX, t % NX, m // NC, m % NC
    zh, zl = z // NL, z % NL
    sends = []

    def at(zz, xx, yy, cc):
        return {"tile": zz * NX + xx, "member": yy * NC + cc}

    def plane(dy, dx):
        return at(z, (x + dx) % NX, (y + dy) % NY, c)

    def low(dl, dx=0):
        return at(zh * NL + (zl + dl) % NL, (x + dx) % NX, y, c)

    def high(dh):
        return at((zh + dh) % NH * NL + zl, x, y, c)

    def member(index):
        return at(z, x, (y + index // NC) % NY, (c + index) % NC)

    def remote(src, dst, name, index, target):
        return pltpu.make_async_remote_copy(
            src_ref=src,
            dst_ref=dst,
            send_sem=sems[name][0].at[index],
            recv_sem=sems[name][1].at[index],
            device_id=target,
            device_id_type=MESH,
        )

    def send(*copy):
        made = remote(*copy)
        made.start()
        sends.append(made)
        return made

    left = {"tile": (t + NZ * NX - 1) % (NZ * NX), "member": m}
    right = {"tile": (t + 1) % (NZ * NX), "member": m}
    sibling = at(z, x, y, 1 - c)

    barrier = pltpu.get_barrier_semaphore()

    def greet(target):
        pl.semaphore_signal(barrier, inc=1, device_id=target, device_id_type=MESH)

    for dh in range(1, NH):
        greet(high(dh))
    greet(left)
    greet(right)
    greet(sibling)
    for step in range(1, 16):
        greet(plane(step // 4, step % 4))
    for dy in range(1, NY):
        greet(at(z, x, (y + dy) % NY, 1 - c))
    for dl in range(1, NL):
        for dx in range(NX):
            greet(low(dl, dx))

    def live(s):
        return jnp.where(s < r.count[0], 1.0, 0.0).astype(F32)

    def place(grid, values):
        grid[...] = jnp.zeros_like(grid)

        @pl.loop(0, GY)
        def _(g):
            found, weight = jnp.int32(0), jnp.float32(0.0)
            for s in range(SLOTS):
                hit = jnp.where(r.lats[0, s] == g, 1, 0)
                found += hit * s
                weight += hit.astype(F32) * live(s)
            tile = values[jnp.minimum(found, SLOTS - 1)].astype(F32) * weight
            grid[pl.ds(REACH + g * TH, TH), LEFT:LEFT + TW, :] = tile

    def send_edges(grid, out, landing, name):
        for row in range(ROWS):
            spot = slice(3 * row, 3 * row + 3)
            r.edge[0, spot, :] = grid[REACH + row, LEFT:LEFT + 3, :]
            r.edge[1, spot, :] = grid[REACH + row, LEFT + TW - 3:LEFT + TW, :]
        out[...] = r.edge[...].astype(BF16)

    def edge_copies(out, landing, name):
        return (
            (out.at[0], landing.at[1], name, 0, left),
            (out.at[1], landing.at[0], name, 1, right),
        )

    def take_edges(grid, landing):
        r.edge[...] = landing[...].astype(F32)
        for row in range(ROWS):
            spot = slice(3 * row, 3 * row + 3)
            grid[REACH + row, LEFT - 3:LEFT, :] = r.edge[0, spot, :]
            grid[REACH + row, LEFT + TW:LEFT + TW + 3, :] = r.edge[1, spot, :]

    def depthwise(grid, s, flipped):
        base = r.lats[0, s] * TH
        total = [jnp.zeros((TW, 256), F32) for _ in range(TH)]
        for b in range(KS):
            for i in range(TH + 2 * REACH):
                window = grid[base + i, LEFT - REACH + b:LEFT - REACH + b + TW, :]
                for a in range(KS):
                    if 0 <= i - a < TH:
                        ka, kb = (KS - 1 - a, KS - 1 - b) if flipped else (a, b)
                        total[i - a] += window * r.kernel[ka, kb:kb + 1, :]
        return total

    r.bias_own[...] = jnp.broadcast_to(r.b_in[...].astype(F32), (8, 128))
    lanes = pl.ds(pl.multiple_of(c * 128, 128), 128)
    other_lanes = pl.ds(pl.multiple_of((1 - c) * 128, 128), 128)
    r.wi[y, :, lanes] = r.w_in[...]
    r.wo[y, lanes, :] = r.w_out[...]
    r.bias[y, :, lanes] = r.bias_own[...]
    place(r.grid_x, r.cells)
    send_edges(r.grid_x, r.edge_x_out, r.edge_x_in, "ex")

    pl.semaphore_wait(barrier, PEERS)

    edges = [send(*copy) for copy in edge_copies(r.edge_x_out, r.edge_x_in, "ex")]

    def weights(yy):
        return (
            r.wi.at[yy, :, lanes],
            r.wo.at[yy, lanes, :],
            r.bias.at[yy, :, lanes],
        )

    def weights_other(yy):
        return (
            r.wi.at[yy, :, other_lanes],
            r.wo.at[yy, other_lanes, :],
            r.bias.at[yy, :, other_lanes],
        )

    for dy in (2, 1, 3):
        for kind, part in enumerate(weights(y)):
            send(part, part, "wy", (dy - 1) * 3 + kind, plane(dy, 0))
    for kind, part in enumerate(weights(y)):
        send(part, part, "wc", kind, sibling)

    def forward_weights(dy):
        yy = (y + NY - dy) % NY
        for kind, part in enumerate(weights(yy)):
            remote(part, part, "wy", (dy - 1) * 3 + kind, plane(dy, 0)).wait_recv()
            send(part, part, "wc", dy * 3 + kind, sibling)

    for s in range(SLOTS):
        r.d_branch[s] = (
            r.cot[s].astype(F32) * (r.scale[...] * live(s))
        ).astype(BF16)
    r.branch[...] = jnp.zeros_like(r.branch)
    r.d_normed[...] = jnp.zeros_like(r.d_normed)

    for copy in edges:
        copy.wait_recv()
    take_edges(r.grid_x, r.edge_x_in)
    forward_weights(1)
    forward_weights(3)

    @pl.loop(0, SLOTS)
    def _(s):
        total = depthwise(r.grid_x, s, False)
        for row in range(TH):
            center = total[row] - jnp.mean(total[row], axis=-1, keepdims=True)
            inverse = lax.rsqrt(jnp.mean(center * center, axis=-1, keepdims=True) + EPSILON)
            normed = center * inverse
            r.normed[s, row] = normed
            r.inverse[s, row] = jnp.broadcast_to(inverse, (TW, 128))
            r.scaled[s, row] = (normed * r.gain[...]).astype(BF16)

    forward_weights(2)

    def pair(dy):
        yy = (y + NY - dy) % NY
        for kind, part in enumerate(weights_other(yy)):
            remote(part, part, "wc", dy * 3 + kind, sibling).wait_recv()
        scaled = r.scaled[...].reshape(256, 256)
        d_branch = r.d_branch[...].reshape(256, 256)
        hidden = dot(scaled, r.wi[yy], (1, 0)) + r.bias[yy, 0:1, :]
        active, derivative = gelu_parts(hidden)
        active = active.astype(BF16)
        r.branch[...] += dot(active, r.wo[yy], (1, 0))
        r.g_out[dy] = dot(active, d_branch, (0, 0)).astype(BF16)
        d_active = dot(d_branch, r.wo[yy], (1, 1))
        d_hidden = (d_active * derivative).astype(BF16)
        r.g_in[dy] = dot(scaled, d_hidden, (0, 0)).astype(BF16)
        to_core = [
            send(r.g_in.at[dy, :, other_lanes], r.core_in.at[dy], "gc", dy * 2, sibling),
            send(r.g_out.at[dy, other_lanes, :], r.core_out.at[dy], "gc", dy * 2 + 1, sibling),
        ]
        r.d_normed[...] += dot(d_hidden, r.wi[yy], (1, 1))
        return to_core

    def spread(dy, to_core):
        back = (NY - dy) % NY
        to_core[0].wait_recv()
        g_in = r.g_in[dy, :, lanes].astype(F32) + r.core_in[dy].astype(F32)
        r.piece[dy, 0] = g_in[:128].astype(BF16)
        r.piece[dy, 1] = g_in[128:].astype(BF16)
        to_core[1].wait_recv()
        g_out = r.g_out[dy, lanes, :].astype(F32) + r.core_out[dy].astype(F32)
        r.piece[dy, 2] = g_out[:, :128].astype(BF16)
        r.piece[dy, 3] = g_out[:, 128:].astype(BF16)
        for dx in (2, 1, 3, 0):
            if dy or dx:
                index = back * 4 + dx
                send(r.piece.at[dy, (x + dx) % NX], r.piece_in.at[index], "gp", index, plane(back, dx))

    held = None
    for dy in ORDER:
        now = (dy, pair(dy))
        if held is not None:
            spread(*held)
        held = now

    for s in range(SLOTS):
        d_normed = r.d_normed[s * 64:(s + 1) * 64, :] * r.gain[...]
        normed = r.normed[s].reshape(64, 256)
        mean = jnp.mean(d_normed, axis=-1, keepdims=True)
        along = jnp.mean(d_normed * normed, axis=-1, keepdims=True)
        inverse = r.inverse[s].reshape(64, 128)[:, 0:1]
        d_conv = inverse * (d_normed - mean - normed * along)
        r.d_conv[s] = d_conv.astype(BF16).astype(F32).reshape(TH, TW, 256)
    place(r.grid_d, r.d_conv)
    send_edges(r.grid_d, r.edge_d_out, r.edge_d_in, "ed")
    edges = [send(*copy) for copy in edge_copies(r.edge_d_out, r.edge_d_in, "ed")]
    spread(*held)

    for b in range(KS):
        def slot_taps(s, sums):
            sums = list(sums)
            base = r.lats[0, s] * TH
            for i in range(TH + 2 * REACH):
                window = r.grid_x[base + i, LEFT - REACH + b:LEFT - REACH + b + TW, :]
                for a in range(KS):
                    if 0 <= i - a < TH:
                        product = window * r.d_conv[s, i - a]
                        sums[a] += product[:8] + product[8:]
            return tuple(sums)

        sums = lax.fori_loop(
            0, SLOTS, slot_taps, tuple(jnp.zeros((8, 256), F32) for _ in range(KS))
        )
        for a in range(KS):
            line = jnp.sum(sums[a], axis=0, keepdims=True)
            for half in range(2):
                at_row = 2 * (a * KS + b) + half
                owner = at_row // 16
                r.taps[owner % NC, owner // NC, at_row % 16:at_row % 16 + 1, :] = (
                    line[:, half * 128:(half + 1) * 128]
                )
    for at_row in range(2 * KS * KS, 128):
        owner = at_row // 16
        r.taps[owner % NC, owner // NC, at_row % 16:at_row % 16 + 1, :] = jnp.zeros((1, 128), F32)
    k_core = send(r.taps.at[1 - c], r.taps_core, "kc", 0, sibling)
    for s in range(SLOTS):
        r.blocked[s] = (
            (r.cells[s].astype(F32) + r.scale[...] * r.branch[s * 64:(s + 1) * 64, :].reshape(TH, TW, 256))
            * live(s)
        ).astype(BF16)
    k_core.wait_recv()
    r.taps_sum[...] = r.taps[c] + r.taps_core[...]
    spot = y * NX + x
    r.taps_plane[spot] = r.taps_sum[y]
    for step in range(1, 16):
        dy, dx = step // 4, step % 4
        send(r.taps_sum.at[(y + dy) % NY], r.taps_plane.at[spot], "kp", step, plane(dy, dx))

    own = r.piece[0, x].astype(F32)
    for step in range(1, 16):
        remote(
            r.piece.at[0, 0], r.piece_in.at[step], "gp", step, plane(step // 4, step % 4)
        ).wait_recv()
        own += r.piece_in[step].astype(F32)
    r.low_out[...] = own.astype(BF16).reshape(NL, 32, 128)
    for dl in (2, 1, 3):
        send(r.low_out.at[(zl + dl) % NL], r.low_in.at[dl], "gl", dl, low(dl))

    for copy in edges:
        copy.wait_recv()
    take_edges(r.grid_d, r.edge_d_in)

    for step in range(1, 16):
        dy, dx = step // 4, step % 4
        origin = (y + NY - dy) % NY * NX + (x + NX - dx) % NX
        remote(r.taps_sum.at[0], r.taps_plane.at[origin], "kp", step, plane(dy, dx)).wait_recv()
    r.taps_low[zl] = jnp.sum(r.taps_plane[...], axis=0)
    for dl in (2, 1, 3):
        send(r.taps_low.at[zl], r.taps_low.at[zl], "kl", dl, low(dl))

    own = r.low_out[zl].astype(F32)
    for dl in range(1, NL):
        remote(r.low_out.at[0], r.low_in.at[dl], "gl", dl, low(dl)).wait_recv()
        own += r.low_in[dl].astype(F32)
    r.high[zh] = own.astype(BF16)
    for dh in (2, 1, 3):
        send(r.high.at[zh], r.high.at[zh], "gh", dh, high(dh))

    @pl.loop(0, SLOTS)
    def _(s):
        total = depthwise(r.grid_d, s, True)
        for row in range(TH):
            r.cell_grad[s, row] = (
                (r.cot[s, row].astype(F32) + total[row]) * live(s)
            ).astype(BF16)

    for dl in range(1, NL):
        origin = (zl + NL - dl) % NL
        remote(r.taps_low.at[0], r.taps_low.at[origin], "kl", dl, low(dl)).wait_recv()
    r.taps_high[zh] = jnp.sum(r.taps_low[...], axis=0)
    for dh in (2, 1, 3):
        send(r.taps_high.at[zh], r.taps_high.at[zh], "kh", dh, high(dh))

    for dh in range(1, NH):
        origin = (zh + NH - dh) % NH
        remote(r.high.at[0], r.high.at[origin], "gh", dh, high(dh)).wait_recv()
    r.full[x, zl] = (jnp.sum(r.high[...].astype(F32), axis=0) * factor).astype(BF16)
    for step in range(1, 16):
        dl, dx = step // 4, step % 4
        send(r.full.at[x, zl], r.full.at[x, zl], "gg", step, low(dl, dx))

    for dh in range(1, NH):
        origin = (zh + NH - dh) % NH
        remote(r.taps_high.at[0], r.taps_high.at[origin], "kh", dh, high(dh)).wait_recv()
    r.taps_full[m] = jnp.sum(r.taps_high[...], axis=0) * factor
    for index in range(1, 8):
        send(r.taps_full.at[m], r.taps_full.at[m], "km", index, member(index))

    for step in range(1, 16):
        dl, dx = step // 4, step % 4
        remote(
            r.full.at[0, 0],
            r.full.at[(x + NX - dx) % NX, (zl + NL - dl) % NL],
            "gg",
            step,
            low(dl, dx),
        ).wait_recv()
    for half in range(2):
        r.grad_in[half * 128:(half + 1) * 128, :] = r.full[half].reshape(128, 128).astype(F32)
        r.grad_out[:, half * 128:(half + 1) * 128] = (
            r.full[2 + half].reshape(128, 128).astype(F32)
        )
    for index in range(1, 8):
        origin = (y + NY - index // NC) % NY * NC + (c + index) % NC
        remote(r.taps_full.at[0], r.taps_full.at[origin], "km", index, member(index)).wait_recv()
    for a in range(KS):
        for b in range(KS):
            for half in range(2):
                at_row = 2 * (a * KS + b) + half
                r.kernel_grad[a, b:b + 1, half * 128:(half + 1) * 128] = (
                    r.taps_full[at_row // 16, at_row % 16:at_row % 16 + 1, :]
                )
    for copy in sends:
        copy.wait_send()


def on_device(
    cells, cotangent, slot_lats, slot_count, kernel, ln_gain, w_in, b_in, w_out, layer_scale
):
    cell_count = 8 * 256 * TH * TW
    factor = 1.0 / math.sqrt(cell_count)
    vmem = pl.BlockSpec(memory_space=pltpu.VMEM)
    smem = pl.BlockSpec(memory_space=pltpu.SMEM)
    tiles = jax.ShapeDtypeStruct((SLOTS, TH, TW, 256), BF16)
    blocked, cell_grad, grad_in, grad_out, kernel_grad = pl.pallas_call(
        functools.partial(block_kernel, factor),
        out_shape=(
            tiles,
            tiles,
            jax.ShapeDtypeStruct((256, 128), F32),
            jax.ShapeDtypeStruct((128, 256), F32),
            jax.ShapeDtypeStruct((KS, KS, 256), F32),
        ),
        in_specs=[vmem, vmem, smem, smem] + [vmem] * 6,
        out_specs=[vmem] * 5,
        scratch_shapes=[pltpu.VMEM(*spec) for spec in VMEM_SCRATCH.values()]
        + [pltpu.SemaphoreType.DMA((n,)) for n in DMA_COUNTS.values() for _ in range(2)],
        compiler_params=pltpu.CompilerParams(
            collective_id=0, has_side_effects=True, vmem_limit_bytes=40 * 1024 * 1024
        ),
        name="block",
    )(
        cells[0],
        cotangent[0],
        slot_lats,
        slot_count,
        kernel,
        ln_gain.reshape(1, 256),
        w_in,
        b_in.reshape(1, 128),
        w_out,
        layer_scale.reshape(1, 256),
    )
    return blocked[None], cell_grad[None], grad_in, grad_out, kernel_grad


def solution(mesh):
    placed = (
        P("member", "tile", None, None, None),
        P("member", "tile", None, None, None),
        P("tile", None),
        P("tile"),
        P(),
        P(),
        P(None, "member"),
        P("member"),
        P("member", None),
        P(),
    )
    return jax.shard_map(
        on_device,
        mesh=mesh,
        in_specs=placed,
        out_specs=(
            P("member", "tile", None, None, None),
            P("member", "tile", None, None, None),
            P(None, "member"),
            P("member", None),
            P(),
        ),
        check_vma=False,
    )
```

time: 667 us -> 69.9 us (0.10)
  waiting for transfers between devices: 466 us -> 0 us
  blocking collectives: 137 us -> 0 us
  Pallas kernels: 0 us -> 60 us
  starting transfers between devices: 25 us -> 0 us
  between operations: 17.6 us -> 1.33 us
  other arithmetic: 11.3 us -> 0 us
    psum x1 -> x0, waiting for transfers between devices: 466 us -> none  [on_device(): lax.psum((grad_in, grad_out, kernel_grad), ('tile', 'member'))]
    psum x1 -> x0, blocking collectives: 99.9 us -> none  [on_device(): lax.psum((grad_in, grad_out, kernel_grad), ('tile', 'member'))]
    pallas_call x0 -> x1, Pallas kernels: none -> 60 us  [on_device(): pl.pallas_call(functools.partial(block_kernel, factor), out_shape=(tiles,...]
    all_gather x3 -> x0, blocking collectives: 36.9 us -> none  [the longest x1 14.1 us: on_device(): lax.all_gather(w_in, 'member', axis=1, tiled=True)]
    ppermute x4 -> x0, starting transfers between devices: 25 us -> none  [the longest x2 19 us: padded_2(): after = lax.ppermute(initial, axis, down)]
  transfers between devices with their start and end apart: 5 -> 0, of which waited for: 2 -> 0; matrix products, arithmetic and copies ran while one was open for 1% -> 0% of each run, Pallas kernels for 0% -> 0%
where the time goes in v1:
time: 69.9 us; the launch traced here: 69.6 us
  Pallas kernels  60 us (86%)
  local copies, waits for them, and re-layouts  8.23 us (12%)
  between operations  1.33 us (2%)
    pallas_call x1, Pallas kernels, on_device(): pl.pallas_call(functools.partial(block_kernel, factor), out_shape=(tiles,...  60 us
    unnamed x23, local copies, waits for them, and re-layouts  8.23 us

profile of v1, /device:TPU:1, one launch (start us, length us, event | category | flops | bytes accessed | tf_op | source)
XLA Modules:
  0.0 69.6 jit_solution(10082806322064220144)
XLA Ops:
  1.3 0.0 copy-start.6
  1.3 0.0 copy-start.8
  1.3 0.0 copy-start.5
  1.3 0.0 copy-start.7
  1.3 0.6 copy-done.6
  2.0 0.0 copy-done.8
  2.0 0.0 copy-done.5
  2.0 0.0 copy-done.7
  2.0 0.0 copy-start
  2.0 0.9 %copy-done = bf16[1,4,4,16,256]{4,3,2,1,0:T(8,128)(2,1)S(1)} copy-done((bf16[1,4,4,16,256]{4,3,2,1,0:T(8,128)(2,1)S(1)}, bf16[1,4,4,16,256]{4,3,2,1,0:T(8,128)(2,1)}, u32[]{:S(2)}) %copy-start) | copy-done | bytes 131096
  2.9 0.0 copy-start.1
  2.9 0.9 %copy-done.1 = bf16[1,4,4,16,256]{4,3,2,1,0:T(8,128)(2,1)S(1)} copy-done((bf16[1,4,4,16,256]{4,3,2,1,0:T(8,128)(2,1)S(1)}, bf16[1,4,4,16,256]{4,3,2,1,0:T(8,128)(2,1)}, u32[]{:S(2)}) %copy-start.1) | copy-done | bytes 131096
  3.8 0.0 copy-start.2
  3.8 0.8 %copy-done.2 = bf16[256,128]{1,0:T(8,128)(2,1)S(1)} copy-done((bf16[256,128]{1,0:T(8,128)(2,1)S(1)}, bf16[256,128]{1,0:T(8,128)(2,1)}, u32[]{:S(2)}) %copy-start.2) | copy-done | bytes 65560
  4.6 0.0 copy-start.3
  4.6 0.8 %copy-done.3 = bf16[128,256]{1,0:T(8,128)(2,1)S(1)} copy-done((bf16[128,256]{1,0:T(8,128)(2,1)S(1)}, bf16[128,256]{1,0:T(8,128)(2,1)}, u32[]{:S(2)}) %copy-start.3) | copy-done | bytes 65560
  5.5 0.0 copy-start.4
  5.5 0.8 %copy-done.4 = f32[7,7,256]{2,1,0:T(8,128)S(1)} copy-done((f32[7,7,256]{2,1,0:T(8,128)S(1)}, f32[7,7,256]{2,1,0:T(8,128)}, u32[]{:S(2)}) %copy-start.4) | copy-done | bytes 50200
  6.3 60.0 %block.1 = (bf16[4,4,16,256]{3,2,1,0:T(8,128)(2,1)S(1)}, bf16[4,4,16,256]{3,2,1,0:T(8,128)(2,1)S(1)}, f32[256,128]{1,0:T(8,128)S(1)}, f32[128,256]{1,0:T(8,128)S(1)}, f32[7,7,256]{2,1,0:T(8,128)S(1)}) custom-call(bf16[4,4,16,256]{3,2,1,0:T(8,128)(2,1)S(1)} %bitcast.9, bf16[4,4,16,256]{3,2,1,0:T(8,128)(2,1)S(1)} %bitcast.10, s32[1,4]{1,0:T(1,128)S(1)} %copy-done.7, ...), custom_call_target="tpu_custom_call" | custom-call | tf_op jit(solution)/shard_map/block/pallas_call | solution.py:456
  66.4 0.7 copy.21
  67.0 0.7 copy.22
  67.7 0.7 copy.23
  68.3 0.7 copy.24
  69.0 0.6 copy.25
Async XLA Ops:
  1.3 0.7 copy-start.6
  1.3 0.7 copy-start.8
  1.3 0.7 copy-start.5
  1.3 0.7 copy-start.7
  2.0 0.9 %copy-start = (bf16[1,4,4,16,256]{4,3,2,1,0:T(8,128)(2,1)S(1)}, bf16[1,4,4,16,256]{4,3,2,1,0:T(8,128)(2,1)}, u32[]{:S(2)}) copy-start(bf16[1,4,4,16,256]{4,3,2,1,0:T(8,128)(2,1)} %param.10) | copy-start | bytes 393220
  2.9 0.9 %copy-start.1 = (bf16[1,4,4,16,256]{4,3,2,1,0:T(8,128)(2,1)S(1)}, bf16[1,4,4,16,256]{4,3,2,1,0:T(8,128)(2,1)}, u32[]{:S(2)}) copy-start(bf16[1,4,4,16,256]{4,3,2,1,0:T(8,128)(2,1)} %param.11) | copy-start | bytes 393220
  3.8 0.8 %copy-start.2 = (bf16[256,128]{1,0:T(8,128)(2,1)S(1)}, bf16[256,128]{1,0:T(8,128)(2,1)}, u32[]{:S(2)}) copy-start(bf16[256,128]{1,0:T(8,128)(2,1)} %refs_6_.1) | copy-start | bytes 196612
  4.6 0.8 %copy-start.3 = (bf16[128,256]{1,0:T(8,128)(2,1)S(1)}, bf16[128,256]{1,0:T(8,128)(2,1)}, u32[]{:S(2)}) copy-start(bf16[128,256]{1,0:T(8,128)(2,1)} %refs_8_.1) | copy-start | bytes 196612
  5.5 0.8 %copy-start.4 = (f32[7,7,256]{2,1,0:T(8,128)S(1)}, f32[7,7,256]{2,1,0:T(8,128)}, u32[]{:S(2)}) copy-start(f32[7,7,256]{2,1,0:T(8,128)} %refs_4_.1) | copy-start | bytes 150532

commit v2 on v1

--- a/solution.py
+++ b/solution.py
@@ -17,10 +17,23 @@
 EPSILON = 1e-06
 MESH = pl.DeviceIdType.MESH
 F32, BF16 = jnp.float32, jnp.bfloat16
-ORDER = (0, 1, 3, 2)
-PEERS = 1 + 15 + 3 + 3 + 3 + 9 + 2
+ORDER = (1, 3, 2, 0)
+PEERS = 6 + 2 + 6 + 3 + 1
 
 VMEM_SCRATCH = dict(
+    cells=((SLOTS, TH, TW, 256), BF16),
+    cot=((SLOTS, TH, TW, 256), BF16),
+    kernel=((KS, KS, 256), F32),
+    w_in=((256, 128), BF16),
+    w_out=((128, 256), BF16),
+    blocked=((SLOTS, TH, TW, 256), BF16),
+    cell_grad=((SLOTS, TH, TW, 256), BF16),
+    grad_in=((256, 128), F32),
+    grad_out=((128, 256), F32),
+    kernel_grad=((KS, KS, 256), F32),
+    strip=((ROWS + 2 * REACH, 16, 256), F32),
+    pair_taps=((KS, REACH, 8, 256), F32),
+    conv=((SLOTS, TH, TW, 256), F32),
     grid_x=((ROWS + 2 * REACH, 32, 256), F32),
     grid_d=((ROWS + 2 * REACH, 32, 256), F32),
     edge=((2, 96, 256), F32),
@@ -61,9 +74,11 @@
     ex=2, ed=2, wy=9, wc=12, gc=8, gp=16, gl=4, gh=4, gg=16, kc=1, kp=16, kl=4, kh=4, km=8
 )
 INPUTS = (
-    "cells", "cot", "lats", "count", "kernel", "gain", "w_in", "b_in", "w_out", "scale"
+    "cells_far", "cot_far", "lats", "count", "kernel_far", "gain", "w_in_far", "b_in", "w_out_far", "scale"
 )
+LOCAL = ("cells", "w_in", "w_out", "kernel", "cot")
 OUTPUTS = ("blocked", "cell_grad", "grad_in", "grad_out", "kernel_grad")
+VMEM_BYTES = 62 * 1024 * 1024
 
 
 class Refs:
@@ -82,13 +97,30 @@
 
 def block_kernel(factor, *refs):
     r = Refs()
-    names = INPUTS + OUTPUTS + tuple(VMEM_SCRATCH)
+    names = INPUTS + tuple(name + "_far" for name in OUTPUTS) + tuple(VMEM_SCRATCH)
     for name, ref in zip(names, refs):
         setattr(r, name, ref)
     sems = {}
     rest = refs[len(names):]
     for index, name in enumerate(DMA_COUNTS):
         sems[name] = (rest[2 * index], rest[2 * index + 1])
+    local_sems, result_sems, relay_1, relay_2 = rest[2 * len(DMA_COUNTS):]
+    local = {}
+    for index, name in enumerate(LOCAL):
+        local[name] = pltpu.make_async_copy(
+            getattr(r, name + "_far"), getattr(r, name), local_sems.at[index]
+        )
+        local[name].start()
+    results = []
+
+    def give(index):
+        name = OUTPUTS[index]
+        copy = pltpu.make_async_copy(
+            getattr(r, name), getattr(r, name + "_far"), result_sems.at[index]
+        )
+        copy.start()
+        results.append(copy)
+
 
     t, m = lax.axis_index("tile"), lax.axis_index("member")
     z, x, y, c = t // NX, t % NX, m // NC, m % NC
@@ -135,18 +167,23 @@
     def greet(target):
         pl.semaphore_signal(barrier, inc=1, device_id=target, device_id_type=MESH)
 
-    for dh in range(1, NH):
-        greet(high(dh))
+    def along(dz):
+        return at((z + NZ + dz) % NZ, x, y, c)
+
+    for dz in (3, -3, 2, -2, 1, -1):
+        greet(along(dz))
     greet(left)
     greet(right)
+    for dy in range(1, NY):
+        greet(plane(dy, 0))
+        greet(at(z, x, (y + dy) % NY, 1 - c))
+    for dx in range(1, NX):
+        greet(plane(0, dx))
     greet(sibling)
-    for step in range(1, 16):
-        greet(plane(step // 4, step % 4))
-    for dy in range(1, NY):
-        greet(at(z, x, (y + dy) % NY, 1 - c))
-    for dl in range(1, NL):
-        for dx in range(NX):
-            greet(low(dl, dx))
+
+    def relay(semaphore, targets):
+        for target in targets:
+            pl.semaphore_signal(semaphore, inc=1, device_id=target, device_id_type=MESH)
 
     def live(s):
         return jnp.where(s < r.count[0], 1.0, 0.0).astype(F32)
@@ -199,13 +236,22 @@
     r.bias_own[...] = jnp.broadcast_to(r.b_in[...].astype(F32), (8, 128))
     lanes = pl.ds(pl.multiple_of(c * 128, 128), 128)
     other_lanes = pl.ds(pl.multiple_of((1 - c) * 128, 128), 128)
+    r.bias[y, :, lanes] = r.bias_own[...]
+    local["cells"].wait()
+    place(r.grid_x, r.cells)
+    send_edges(r.grid_x, r.edge_x_out, r.edge_x_in, "ex")
+
+    local["w_in"].wait()
+    local["w_out"].wait()
     r.wi[y, :, lanes] = r.w_in[...]
     r.wo[y, lanes, :] = r.w_out[...]
-    r.bias[y, :, lanes] = r.bias_own[...]
-    place(r.grid_x, r.cells)
-    send_edges(r.grid_x, r.edge_x_out, r.edge_x_in, "ex")
-
     pl.semaphore_wait(barrier, PEERS)
+    relay(
+        relay_1,
+        [plane(dy, 0) for dy in range(1, NY)]
+        + [plane(0, dx) for dx in range(1, NX)]
+        + [along(2), along(-2)],
+    )
 
     edges = [send(*copy) for copy in edge_copies(r.edge_x_out, r.edge_x_in, "ex")]
 
@@ -223,7 +269,7 @@
             r.bias.at[yy, :, other_lanes],
         )
 
-    for dy in (2, 1, 3):
+    for dy in (1, 3, 2):
         for kind, part in enumerate(weights(y)):
             send(part, part, "wy", (dy - 1) * 3 + kind, plane(dy, 0))
     for kind, part in enumerate(weights(y)):
@@ -235,6 +281,22 @@
             remote(part, part, "wy", (dy - 1) * 3 + kind, plane(dy, 0)).wait_recv()
             send(part, part, "wc", dy * 3 + kind, sibling)
 
+    local["kernel"].wait()
+    low_half = lax.broadcasted_iota(jnp.int32, (8, 256), 0) < 4
+    for a in range(KS):
+        for b in range(REACH):
+            r.pair_taps[a, b] = jnp.where(
+                low_half, r.kernel[a, b:b + 1, :], r.kernel[a, b + 4:b + 5, :]
+            )
+
+    @pl.loop(0, SLOTS)
+    def _(s):
+        total = depthwise(r.grid_x, s, False)
+        for row in range(TH):
+            r.conv[s, row] = total[row]
+
+    r.strip[...] = jnp.zeros_like(r.strip)
+    local["cot"].wait()
     for s in range(SLOTS):
         r.d_branch[s] = (
             r.cot[s].astype(F32) * (r.scale[...] * live(s))
@@ -242,24 +304,40 @@
     r.branch[...] = jnp.zeros_like(r.branch)
     r.d_normed[...] = jnp.zeros_like(r.d_normed)
 
+    pl.semaphore_wait(relay_1, 8)
+    relay(
+        relay_2, [plane(0, dx) for dx in range(1, NX)] + [along(4), along(-4)]
+    )
     for copy in edges:
         copy.wait_recv()
-    take_edges(r.grid_x, r.edge_x_in)
+    r.edge[...] = r.edge_x_in[...].astype(F32)
+    for row in range(ROWS):
+        spot = slice(3 * row, 3 * row + 3)
+        r.strip[REACH + row, 0:3, :] = r.edge[0, spot, :]
+        r.strip[REACH + row, 7:10, :] = r.edge[1, spot, :]
     forward_weights(1)
     forward_weights(3)
 
     @pl.loop(0, SLOTS)
     def _(s):
-        total = depthwise(r.grid_x, s, False)
+        base = r.lats[0, s] * TH
+        outer = [jnp.zeros((8, 256), F32) for _ in range(TH)]
+        for b in range(REACH):
+            for i in range(TH + 2 * REACH):
+                window = r.strip[base + i, b:b + 8, :]
+                for a in range(KS):
+                    if 0 <= i - a < TH:
+                        outer[i - a] += window * r.pair_taps[a, b]
         for row in range(TH):
-            center = total[row] - jnp.mean(total[row], axis=-1, keepdims=True)
+            total = r.conv[s, row] + jnp.concatenate(
+                [jnp.where(low_half, outer[row], 0.0), jnp.where(low_half, 0.0, outer[row])], axis=0
+            )
+            center = total - jnp.mean(total, axis=-1, keepdims=True)
             inverse = lax.rsqrt(jnp.mean(center * center, axis=-1, keepdims=True) + EPSILON)
             normed = center * inverse
             r.normed[s, row] = normed
             r.inverse[s, row] = jnp.broadcast_to(inverse, (TW, 128))
             r.scaled[s, row] = (normed * r.gain[...]).astype(BF16)
-
-    forward_weights(2)
 
     def pair(dy):
         yy = (y + NY - dy) % NY
@@ -297,9 +375,12 @@
                 index = back * 4 + dx
                 send(r.piece.at[dy, (x + dx) % NX], r.piece_in.at[index], "gp", index, plane(back, dx))
 
+    pl.semaphore_wait(relay_2, 5)
     held = None
     for dy in ORDER:
         now = (dy, pair(dy))
+        if dy == 1:
+            forward_weights(2)
         if held is not None:
             spread(*held)
         held = now
@@ -317,6 +398,7 @@
     edges = [send(*copy) for copy in edge_copies(r.edge_d_out, r.edge_d_in, "ed")]
     spread(*held)
 
+    take_edges(r.grid_x, r.edge_x_in)
     for b in range(KS):
         def slot_taps(s, sums):
             sums = list(sums)
@@ -349,6 +431,7 @@
             (r.cells[s].astype(F32) + r.scale[...] * r.branch[s * 64:(s + 1) * 64, :].reshape(TH, TW, 256))
             * live(s)
         ).astype(BF16)
+    give(0)
     k_core.wait_recv()
     r.taps_sum[...] = r.taps[c] + r.taps_core[...]
     spot = y * NX + x
@@ -395,6 +478,7 @@
                 (r.cot[s, row].astype(F32) + total[row]) * live(s)
             ).astype(BF16)
 
+    give(1)
     for dl in range(1, NL):
         origin = (zl + NL - dl) % NL
         remote(r.taps_low.at[0], r.taps_low.at[origin], "kl", dl, low(dl)).wait_recv()
@@ -431,6 +515,8 @@
         r.grad_out[:, half * 128:(half + 1) * 128] = (
             r.full[2 + half].reshape(128, 128).astype(F32)
         )
+    give(2)
+    give(3)
     for index in range(1, 8):
         origin = (y + NY - index // NC) % NY * NC + (c + index) % NC
         remote(r.taps_full.at[0], r.taps_full.at[origin], "km", index, member(index)).wait_recv()
@@ -441,8 +527,29 @@
                 r.kernel_grad[a, b:b + 1, half * 128:(half + 1) * 128] = (
                     r.taps_full[at_row // 16, at_row % 16:at_row % 16 + 1, :]
                 )
+    give(4)
     for copy in sends:
         copy.wait_send()
+    for copy in results:
+        copy.wait()
+
+
+def write_kernel(*refs):
+    taken = [
+        pltpu.make_async_copy(refs[index], refs[10 + index], refs[15].at[index])
+        for index in range(5)
+    ]
+    given = [
+        pltpu.make_async_copy(refs[10 + index], refs[5 + index], refs[16].at[index])
+        for index in range(5)
+    ]
+    for copy in taken:
+        copy.start()
+    for index in range(5):
+        taken[index].wait()
+        given[index].start()
+    for copy in given:
+        copy.wait()
 
 
 def on_device(
@@ -452,22 +559,30 @@
     factor = 1.0 / math.sqrt(cell_count)
     vmem = pl.BlockSpec(memory_space=pltpu.VMEM)
     smem = pl.BlockSpec(memory_space=pltpu.SMEM)
+    hbm = pl.BlockSpec(memory_space=pltpu.HBM)
     tiles = jax.ShapeDtypeStruct((SLOTS, TH, TW, 256), BF16)
-    blocked, cell_grad, grad_in, grad_out, kernel_grad = pl.pallas_call(
+    shapes = (
+        tiles,
+        tiles,
+        jax.ShapeDtypeStruct((256, 128), F32),
+        jax.ShapeDtypeStruct((128, 256), F32),
+        jax.ShapeDtypeStruct((KS, KS, 256), F32),
+    )
+    results = pl.pallas_call(
         functools.partial(block_kernel, factor),
-        out_shape=(
-            tiles,
-            tiles,
-            jax.ShapeDtypeStruct((256, 128), F32),
-            jax.ShapeDtypeStruct((128, 256), F32),
-            jax.ShapeDtypeStruct((KS, KS, 256), F32),
-        ),
-        in_specs=[vmem, vmem, smem, smem] + [vmem] * 6,
-        out_specs=[vmem] * 5,
+        out_shape=shapes,
+        in_specs=[hbm, hbm, smem, smem, hbm, vmem, hbm, vmem, hbm, vmem],
+        out_specs=[hbm] * 5,
         scratch_shapes=[pltpu.VMEM(*spec) for spec in VMEM_SCRATCH.values()]
-        + [pltpu.SemaphoreType.DMA((n,)) for n in DMA_COUNTS.values() for _ in range(2)],
+        + [pltpu.SemaphoreType.DMA((n,)) for n in DMA_COUNTS.values() for _ in range(2)]
+        + [
+            pltpu.SemaphoreType.DMA((len(LOCAL),)),
+            pltpu.SemaphoreType.DMA((len(OUTPUTS),)),
+            pltpu.SemaphoreType.REGULAR,
+            pltpu.SemaphoreType.REGULAR,
+        ],
         compiler_params=pltpu.CompilerParams(
-            collective_id=0, has_side_effects=True, vmem_limit_bytes=40 * 1024 * 1024
+            collective_id=0, has_side_effects=True, vmem_limit_bytes=VMEM_BYTES
         ),
         name="block",
     )(
@@ -482,6 +597,16 @@
         w_out,
         layer_scale.reshape(1, 256),
     )
+    blocked, cell_grad, grad_in, grad_out, kernel_grad = pl.pallas_call(
+        write_kernel,
+        out_shape=shapes,
+        in_specs=[hbm] * 5,
+        out_specs=[hbm] * 5,
+        scratch_shapes=[pltpu.VMEM(shape.shape, shape.dtype) for shape in shapes]
+        + [pltpu.SemaphoreType.DMA((5,)), pltpu.SemaphoreType.DMA((5,))],
+        compiler_params=pltpu.CompilerParams(vmem_limit_bytes=VMEM_BYTES),
+        name="write",
+    )(*results)
     return blocked[None], cell_grad[None], grad_in, grad_out, kernel_grad
 
 

time: 69.9 us -> 57.2 us (0.82)
  local copies, waits for them, and re-layouts: 8.23 us -> 0 us
  Pallas kernels: 60 us -> 55.8 us
    unnamed x23 -> x0, local copies, waits for them, and re-layouts: 8.23 us -> none
    pallas_call x1 -> x2, Pallas kernels: 60 us -> 55.8 us  [the longest x1 53.9 us: on_device(): pl.pallas_call(functools.partial(block_kernel, factor), out_shape=shapes,...]
where the time goes in v2:
time: 57.2 us; the launch traced here: 57 us
  Pallas kernels  55.8 us (98%)
  between operations  1.29 us (2%)
    pallas_call x1, Pallas kernels, on_device(): pl.pallas_call(functools.partial(block_kernel, factor), out_shape=shapes,...  53.9 us
    pallas_call x1, Pallas kernels, on_device(): pl.pallas_call(write_kernel, out_shape=shapes, in_specs=[hbm] * 5, out_sp...  1.85 us

profile of v2, /device:TPU:1, one launch (start us, length us, event | category | flops | bytes accessed | tf_op | source)
XLA Modules:
  0.0 57.0 jit_solution(6498972342150872514)
XLA Ops:
  1.3 53.9 %block.1 = (bf16[4,4,16,256]{3,2,1,0:T(8,128)(2,1)}, bf16[4,4,16,256]{3,2,1,0:T(8,128)(2,1)}, f32[256,128]{1,0:T(8,128)}, f32[128,256]{1,0:T(8,128)}, f32[7,7,256]{2,1,0:T(8,128)}) custom-call(bf16[4,4,16,256]{3,2,1,0:T(8,128)(2,1)} %bitcast.7, bf16[4,4,16,256]{3,2,1,0:T(8,128)(2,1)} %bitcast.8, s32[1,4]{1,0:T(1,128)} %refs_2_.1, s32[1]{0:T(128)S(6)} %copy.15.refs_3_, ...), custom_call_target="tpu_custom_call" | custom-call | tf_op jit(solution)/shard_map/block/pallas_call | solution.py:571
  55.2 1.8 %write.1 = (bf16[4,4,16,256]{3,2,1,0:T(8,128)(2,1)}, bf16[4,4,16,256]{3,2,1,0:T(8,128)(2,1)}, f32[256,128]{1,0:T(8,128)}, f32[128,256]{1,0:T(8,128)}, f32[7,7,256]{2,1,0:T(8,128)}) custom-call(bf16[4,4,16,256]{3,2,1,0:T(8,128)(2,1)} %get-tuple-element.15.refs_0_, bf16[4,4,16,256]{3,2,1,0:T(8,128)(2,1)} %get-tuple-element.16.refs_1_, ...), custom_call_target="tpu_custom_call" | custom-call | tf_op jit(solution)/shard_map/write/pallas_call | solution.py:600

commit v3 on v2

--- a/solution.py
+++ b/solution.py
@@ -17,7 +17,6 @@
 EPSILON = 1e-06
 MESH = pl.DeviceIdType.MESH
 F32, BF16 = jnp.float32, jnp.bfloat16
-ORDER = (1, 3, 2, 0)
 PEERS = 6 + 2 + 6 + 3 + 1
 
 VMEM_SCRATCH = dict(
@@ -28,9 +27,6 @@
     w_out=((128, 256), BF16),
     blocked=((SLOTS, TH, TW, 256), BF16),
     cell_grad=((SLOTS, TH, TW, 256), BF16),
-    grad_in=((256, 128), F32),
-    grad_out=((128, 256), F32),
-    kernel_grad=((KS, KS, 256), F32),
     strip=((ROWS + 2 * REACH, 16, 256), F32),
     pair_taps=((KS, REACH, 8, 256), F32),
     conv=((SLOTS, TH, TW, 256), F32),
@@ -61,14 +57,14 @@
     low_out=((NL, 32, 128), BF16),
     low_in=((NL, 32, 128), BF16),
     high=((NH, 32, 128), BF16),
-    full=((NX, NL, 32, 128), BF16),
+    full_own=((32, 128), BF16),
     taps=((NC, NY, 16, 128), F32),
     taps_core=((NY, 16, 128), F32),
     taps_sum=((NY, 16, 128), F32),
     taps_plane=((NY * NX, 16, 128), F32),
     taps_low=((NL, 16, 128), F32),
     taps_high=((NH, 16, 128), F32),
-    taps_full=((NY * NC, 16, 128), F32),
+    taps_own=((16, 128), F32),
 )
 DMA_COUNTS = dict(
     ex=2, ed=2, wy=9, wc=12, gc=8, gp=16, gl=4, gh=4, gg=16, kc=1, kp=16, kl=4, kh=4, km=8
@@ -77,7 +73,7 @@
     "cells_far", "cot_far", "lats", "count", "kernel_far", "gain", "w_in_far", "b_in", "w_out_far", "scale"
 )
 LOCAL = ("cells", "w_in", "w_out", "kernel", "cot")
-OUTPUTS = ("blocked", "cell_grad", "grad_in", "grad_out", "kernel_grad")
+OUTPUTS = ("blocked", "cell_grad", "full", "taps_full")
 VMEM_BYTES = 62 * 1024 * 1024
 
 
@@ -113,11 +109,8 @@
         local[name].start()
     results = []
 
-    def give(index):
-        name = OUTPUTS[index]
-        copy = pltpu.make_async_copy(
-            getattr(r, name), getattr(r, name + "_far"), result_sems.at[index]
-        )
+    def give(index, source, target):
+        copy = pltpu.make_async_copy(source, target, result_sems.at[index])
         copy.start()
         results.append(copy)
 
@@ -315,8 +308,6 @@
         spot = slice(3 * row, 3 * row + 3)
         r.strip[REACH + row, 0:3, :] = r.edge[0, spot, :]
         r.strip[REACH + row, 7:10, :] = r.edge[1, spot, :]
-    forward_weights(1)
-    forward_weights(3)
 
     @pl.loop(0, SLOTS)
     def _(s):
@@ -375,15 +366,17 @@
                 index = back * 4 + dx
                 send(r.piece.at[dy, (x + dx) % NX], r.piece_in.at[index], "gp", index, plane(back, dx))
 
+    forward_weights(1)
+    forward_weights(3)
     pl.semaphore_wait(relay_2, 5)
-    held = None
-    for dy in ORDER:
-        now = (dy, pair(dy))
-        if dy == 1:
-            forward_weights(2)
-        if held is not None:
-            spread(*held)
-        held = now
+    first = pair(1)
+    second = pair(3)
+    spread(1, first)
+    own_pair = pair(0)
+    spread(3, second)
+    forward_weights(2)
+    spread(0, own_pair)
+    last = pair(2)
 
     for s in range(SLOTS):
         d_normed = r.d_normed[s * 64:(s + 1) * 64, :] * r.gain[...]
@@ -396,7 +389,7 @@
     place(r.grid_d, r.d_conv)
     send_edges(r.grid_d, r.edge_d_out, r.edge_d_in, "ed")
     edges = [send(*copy) for copy in edge_copies(r.edge_d_out, r.edge_d_in, "ed")]
-    spread(*held)
+    spread(2, last)
 
     take_edges(r.grid_x, r.edge_x_in)
     for b in range(KS):
@@ -431,7 +424,7 @@
             (r.cells[s].astype(F32) + r.scale[...] * r.branch[s * 64:(s + 1) * 64, :].reshape(TH, TW, 256))
             * live(s)
         ).astype(BF16)
-    give(0)
+    give(0, r.blocked, r.blocked_far)
     k_core.wait_recv()
     r.taps_sum[...] = r.taps[c] + r.taps_core[...]
     spot = y * NX + x
@@ -470,6 +463,13 @@
     for dh in (2, 1, 3):
         send(r.high.at[zh], r.high.at[zh], "gh", dh, high(dh))
 
+    for dl in range(1, NL):
+        origin = (zl + NL - dl) % NL
+        remote(r.taps_low.at[0], r.taps_low.at[origin], "kl", dl, low(dl)).wait_recv()
+    r.taps_high[zh] = jnp.sum(r.taps_low[...], axis=0)
+    for dh in (2, 1, 3):
+        send(r.taps_high.at[zh], r.taps_high.at[zh], "kh", dh, high(dh))
+
     @pl.loop(0, SLOTS)
     def _(s):
         total = depthwise(r.grid_d, s, True)
@@ -478,76 +478,77 @@
                 (r.cot[s, row].astype(F32) + total[row]) * live(s)
             ).astype(BF16)
 
-    give(1)
-    for dl in range(1, NL):
-        origin = (zl + NL - dl) % NL
-        remote(r.taps_low.at[0], r.taps_low.at[origin], "kl", dl, low(dl)).wait_recv()
-    r.taps_high[zh] = jnp.sum(r.taps_low[...], axis=0)
-    for dh in (2, 1, 3):
-        send(r.taps_high.at[zh], r.taps_high.at[zh], "kh", dh, high(dh))
+    give(1, r.cell_grad, r.cell_grad_far)
+
 
     for dh in range(1, NH):
         origin = (zh + NH - dh) % NH
         remote(r.high.at[0], r.high.at[origin], "gh", dh, high(dh)).wait_recv()
-    r.full[x, zl] = (jnp.sum(r.high[...].astype(F32), axis=0) * factor).astype(BF16)
+    r.full_own[...] = (jnp.sum(r.high[...].astype(F32), axis=0) * factor).astype(BF16)
     for step in range(1, 16):
         dl, dx = step // 4, step % 4
-        send(r.full.at[x, zl], r.full.at[x, zl], "gg", step, low(dl, dx))
+        send(r.full_own, r.full_far.at[x, zl], "gg", step, low(dl, dx))
+    give(2, r.full_own, r.full_far.at[x, zl])
 
     for dh in range(1, NH):
         origin = (zh + NH - dh) % NH
         remote(r.taps_high.at[0], r.taps_high.at[origin], "kh", dh, high(dh)).wait_recv()
-    r.taps_full[m] = jnp.sum(r.taps_high[...], axis=0) * factor
+    r.taps_own[...] = jnp.sum(r.taps_high[...], axis=0) * factor
     for index in range(1, 8):
-        send(r.taps_full.at[m], r.taps_full.at[m], "km", index, member(index))
+        send(r.taps_own, r.taps_full_far.at[m], "km", index, member(index))
+    give(3, r.taps_own, r.taps_full_far.at[m])
 
     for step in range(1, 16):
         dl, dx = step // 4, step % 4
         remote(
-            r.full.at[0, 0],
-            r.full.at[(x + NX - dx) % NX, (zl + NL - dl) % NL],
+            r.full_own,
+            r.full_far.at[(x + NX - dx) % NX, (zl + NL - dl) % NL],
             "gg",
             step,
             low(dl, dx),
         ).wait_recv()
-    for half in range(2):
-        r.grad_in[half * 128:(half + 1) * 128, :] = r.full[half].reshape(128, 128).astype(F32)
-        r.grad_out[:, half * 128:(half + 1) * 128] = (
-            r.full[2 + half].reshape(128, 128).astype(F32)
-        )
-    give(2)
-    give(3)
     for index in range(1, 8):
         origin = (y + NY - index // NC) % NY * NC + (c + index) % NC
-        remote(r.taps_full.at[0], r.taps_full.at[origin], "km", index, member(index)).wait_recv()
+        remote(r.taps_own, r.taps_full_far.at[origin], "km", index, member(index)).wait_recv()
+    for copy in sends:
+        copy.wait_send()
+    for copy in results:
+        copy.wait()
+
+
+def write_kernel(*refs):
+    far, out, near = refs[:4], refs[4:9], refs[9:16]
+    blocked, cell_grad, full, taps, grad_in, grad_out, kernel_grad = near
+    take_sems, give_sems = refs[16:]
+    taken = [
+        pltpu.make_async_copy(far[index], near[index], take_sems.at[index]) for index in range(4)
+    ]
+    given = [
+        pltpu.make_async_copy(source, out[index], give_sems.at[index])
+        for index, source in enumerate((blocked, cell_grad, grad_in, grad_out, kernel_grad))
+    ]
+    for index in (2, 3, 0, 1):
+        taken[index].start()
+    taken[2].wait()
+    for half in range(2):
+        part = slice(half * 128, (half + 1) * 128)
+        grad_in[part, :] = full[half].reshape(128, 128).astype(F32)
+        grad_out[:, part] = full[2 + half].reshape(128, 128).astype(F32)
+    given[2].start()
+    given[3].start()
+    taken[0].wait()
+    given[0].start()
+    taken[1].wait()
+    given[1].start()
+    taken[3].wait()
     for a in range(KS):
         for b in range(KS):
             for half in range(2):
                 at_row = 2 * (a * KS + b) + half
-                r.kernel_grad[a, b:b + 1, half * 128:(half + 1) * 128] = (
-                    r.taps_full[at_row // 16, at_row % 16:at_row % 16 + 1, :]
+                kernel_grad[a, b:b + 1, half * 128:(half + 1) * 128] = (
+                    taps[at_row // 16, at_row % 16:at_row % 16 + 1, :]
                 )
-    give(4)
-    for copy in sends:
-        copy.wait_send()
-    for copy in results:
-        copy.wait()
-
-
-def write_kernel(*refs):
-    taken = [
-        pltpu.make_async_copy(refs[index], refs[10 + index], refs[15].at[index])
-        for index in range(5)
-    ]
-    given = [
-        pltpu.make_async_copy(refs[10 + index], refs[5 + index], refs[16].at[index])
-        for index in range(5)
-    ]
-    for copy in taken:
-        copy.start()
-    for index in range(5):
-        taken[index].wait()
-        given[index].start()
+    given[4].start()
     for copy in given:
         copy.wait()
 
@@ -568,11 +569,17 @@
         jax.ShapeDtypeStruct((128, 256), F32),
         jax.ShapeDtypeStruct((KS, KS, 256), F32),
     )
+    parts = (
+        tiles,
+        tiles,
+        jax.ShapeDtypeStruct((NX, NL, 32, 128), BF16),
+        jax.ShapeDtypeStruct((NY * NC, 16, 128), F32),
+    )
     results = pl.pallas_call(
         functools.partial(block_kernel, factor),
-        out_shape=shapes,
+        out_shape=parts,
         in_specs=[hbm, hbm, smem, smem, hbm, vmem, hbm, vmem, hbm, vmem],
-        out_specs=[hbm] * 5,
+        out_specs=[hbm] * 4,
         scratch_shapes=[pltpu.VMEM(*spec) for spec in VMEM_SCRATCH.values()]
         + [pltpu.SemaphoreType.DMA((n,)) for n in DMA_COUNTS.values() for _ in range(2)]
         + [
@@ -600,10 +607,10 @@
     blocked, cell_grad, grad_in, grad_out, kernel_grad = pl.pallas_call(
         write_kernel,
         out_shape=shapes,
-        in_specs=[hbm] * 5,
+        in_specs=[hbm] * 4,
         out_specs=[hbm] * 5,
-        scratch_shapes=[pltpu.VMEM(shape.shape, shape.dtype) for shape in shapes]
-        + [pltpu.SemaphoreType.DMA((5,)), pltpu.SemaphoreType.DMA((5,))],
+        scratch_shapes=[pltpu.VMEM(shape.shape, shape.dtype) for shape in parts + shapes[2:]]
+        + [pltpu.SemaphoreType.DMA((4,)), pltpu.SemaphoreType.DMA((5,))],
         compiler_params=pltpu.CompilerParams(vmem_limit_bytes=VMEM_BYTES),
         name="write",
     )(*results)

time: 57.2 us -> 55.9 us (0.977)
  Pallas kernels: 55.8 us -> 54.5 us
    pallas_call x2, Pallas kernels: 55.8 us -> 54.5 us  [the longest x1 52.7 us: on_device(): pl.pallas_call(functools.partial(block_kernel, factor), out_shape=parts,...]
where the time goes in v3:
time: 55.9 us; the launch traced here: 55.7 us
  Pallas kernels  54.5 us (97%)
  between operations  1.29 us (2%)
    pallas_call x1, Pallas kernels, on_device(): pl.pallas_call(functools.partial(block_kernel, factor), out_shape=parts,...  52.7 us
    pallas_call x1, Pallas kernels, on_device(): pl.pallas_call(write_kernel, out_shape=shapes, in_specs=[hbm] * 4, out_sp...  1.81 us

profile of v3, /device:TPU:1, one launch (start us, length us, event | category | flops | bytes accessed | tf_op | source)
XLA Modules:
  0.0 55.7 jit_solution(7443757670422320331)
XLA Ops:
  1.3 52.7 %block.1 = (bf16[4,4,16,256]{3,2,1,0:T(8,128)(2,1)}, bf16[4,4,16,256]{3,2,1,0:T(8,128)(2,1)}, bf16[4,4,32,128]{3,2,1,0:T(8,128)(2,1)}, f32[8,16,128]{2,1,0:T(8,128)}) custom-call(bf16[4,4,16,256]{3,2,1,0:T(8,128)(2,1)} %bitcast.7, bf16[4,4,16,256]{3,2,1,0:T(8,128)(2,1)} %bitcast.8, s32[1,4]{1,0:T(1,128)} %refs_2_.1, s32[1]{0:T(128)S(6)} %copy.15.refs_3_, ...), custom_call_target="tpu_custom_call" | custom-call | tf_op jit(solution)/shard_map/block/pallas_call | solution.py:578
  53.9 1.8 %write.1 = (bf16[4,4,16,256]{3,2,1,0:T(8,128)(2,1)}, bf16[4,4,16,256]{3,2,1,0:T(8,128)(2,1)}, f32[256,128]{1,0:T(8,128)}, f32[128,256]{1,0:T(8,128)}, f32[7,7,256]{2,1,0:T(8,128)}) custom-call(bf16[4,4,16,256]{3,2,1,0:T(8,128)(2,1)} %get-tuple-element.14.refs_0_, bf16[4,4,16,256]{3,2,1,0:T(8,128)(2,1)} %get-tuple-element.15.refs_1_, ...), custom_call_target="tpu_custom_call" | custom-call | tf_op jit(solution)/shard_map/write/pallas_call | solution.py:607

commit v4 on v3

--- a/solution.py
+++ b/solution.py
@@ -372,11 +372,11 @@
     first = pair(1)
     second = pair(3)
     spread(1, first)
-    own_pair = pair(0)
     spread(3, second)
     forward_weights(2)
-    spread(0, own_pair)
-    last = pair(2)
+    third = pair(2)
+    last = pair(0)
+    spread(2, third)
 
     for s in range(SLOTS):
         d_normed = r.d_normed[s * 64:(s + 1) * 64, :] * r.gain[...]
@@ -389,7 +389,7 @@
     place(r.grid_d, r.d_conv)
     send_edges(r.grid_d, r.edge_d_out, r.edge_d_in, "ed")
     edges = [send(*copy) for copy in edge_copies(r.edge_d_out, r.edge_d_in, "ed")]
-    spread(2, last)
+    spread(0, last)
 
     take_edges(r.grid_x, r.edge_x_in)
     for b in range(KS):

time: 55.9 us -> 56.6 us (1.013)
  Pallas kernels: 54.5 us -> 55.2 us
    pallas_call x1, Pallas kernels: 52.7 us -> 53.4 us  [on_device(): pl.pallas_call(functools.partial(block_kernel, factor), out_shape=parts,...]
where the time goes in v4:
time: 56.6 us; the launch traced here: 56.5 us
  Pallas kernels  55.2 us (98%)
  between operations  1.29 us (2%)
    pallas_call x1, Pallas kernels, on_device(): pl.pallas_call(functools.partial(block_kernel, factor), out_shape=parts,...  53.4 us
    pallas_call x1, Pallas kernels, on_device(): pl.pallas_call(write_kernel, out_shape=shapes, in_specs=[hbm] * 4, out_sp...  1.81 us

profile of v4, /device:TPU:1, one launch (start us, length us, event | category | flops | bytes accessed | tf_op | source)
XLA Modules:
  0.0 56.5 jit_solution(15049288987237841813)
XLA Ops:
  1.3 53.4 %block.1 = (bf16[4,4,16,256]{3,2,1,0:T(8,128)(2,1)}, bf16[4,4,16,256]{3,2,1,0:T(8,128)(2,1)}, bf16[4,4,32,128]{3,2,1,0:T(8,128)(2,1)}, f32[8,16,128]{2,1,0:T(8,128)}) custom-call(bf16[4,4,16,256]{3,2,1,0:T(8,128)(2,1)} %bitcast.7, bf16[4,4,16,256]{3,2,1,0:T(8,128)(2,1)} %bitcast.8, s32[1,4]{1,0:T(1,128)} %refs_2_.1, s32[1]{0:T(128)S(6)} %copy.15.refs_3_, ...), custom_call_target="tpu_custom_call" | custom-call | tf_op jit(solution)/shard_map/block/pallas_call | solution.py:578
  54.6 1.8 %write.1 = (bf16[4,4,16,256]{3,2,1,0:T(8,128)(2,1)}, bf16[4,4,16,256]{3,2,1,0:T(8,128)(2,1)}, f32[256,128]{1,0:T(8,128)}, f32[128,256]{1,0:T(8,128)}, f32[7,7,256]{2,1,0:T(8,128)}) custom-call(bf16[4,4,16,256]{3,2,1,0:T(8,128)(2,1)} %get-tuple-element.14.refs_0_, bf16[4,4,16,256]{3,2,1,0:T(8,128)(2,1)} %get-tuple-element.15.refs_1_, ...), custom_call_target="tpu_custom_call" | custom-call | tf_op jit(solution)/shard_map/write/pallas_call | solution.py:607
